TPU v7x, 32 devices: a whole 2x2x4 slice. The times are simulated.
32 devices in a mesh: replica: 4 (over y, x), mp: 8 (over z, core).
Axes of the slice: x: 2, y: 2, z: 4, core: 2. Of those that a mesh axis runs over, the one named last changes fastest.
Arguments:
- row_table: float32 [16384, 128], P('mp'), may hold values from -3 to 3
- grad_history: float32 [16384, 128], P('mp'), may hold values from 0.1 to 1
- touched: int32 [4, 8, 8, 256], P('replica', 'mp'), may hold values from 0 to 2047
- lookup_slot: int32 [4, 256, 32, 2], P('replica', None, 'mp'), may hold values from 0 to 2047, as said below
- pool_counts: int32 [4, 256, 32], P('replica', None, 'mp'), may hold values from 1 to 2
- cross_down: bfloat16 [4096, 512], P('mp'), may hold values from -0.09375 to 0.09375
- cross_up: bfloat16 [4096, 512], P('mp'), may hold values from -0.25 to 0.25
- cross_bias: float32 [4096], P('mp'), may hold values from -3 to 3
- cotangent: bfloat16 [4, 256, 4096], P('replica', None, 'mp'), may hold values from -0.59765625 to 0.59765625
Outputs:
- crossed: bfloat16 [4, 256, 4096], P('replica', None, 'mp')
- new_table: float32 [16384, 128], P('mp')
- fresh_history_sums: float32 [16384, 128], P('mp')
Inputs may be any that keep to these rules, and one draw needn't show every extreme that they name: For each group and each mp index m, the entries of lookup_slot over all 256 samples, the 4 features held by m and all 2 lookups are a permutation of 0 to 2047, so every owner receives exactly 256 slots from every mp index.
All inputs are finite; a program needn't handle non-finite values.
Results may differ from a plain program's by a relative error of at most 0.017.
Values may be sent and summed in bfloat16 or wider, within the bound.
A program may use at most 64 MiB of HBM per device.

v0:
```python
import jax
import jax.numpy as jnp
from jax import lax
from jax.sharding import PartitionSpec as P

learn_rate = 0.5
epsilon = 1e-06


def shards(
    row_table,
    grad_history,
    touched,
    lookup_slot,
    pool_counts,
    cross_down,
    cross_up,
    cross_bias,
    cotangent,
):
    row_width = row_table.shape[1]
    wanted = touched[0, 0]
    sending = row_table.astype(jnp.bfloat16)[wanted]
    arrived = lax.all_to_all(sending, "mp", split_axis=0, concat_axis=0, tiled=True)
    arrived_flat = arrived.reshape(-1, row_width)
    slot_index = lookup_slot[0]
    counts = pool_counts[0]
    samples, features, hot_count = slot_index.shape
    picked = arrived_flat[slot_index].astype(jnp.float32)
    live_mask = (jnp.arange(hot_count, dtype=jnp.int32)[None, None, :] < counts[:, :, None]).astype(
        jnp.float32
    )
    divisor = counts.astype(jnp.float32)[:, :, None]
    pooled = (jnp.sum(picked * live_mask[..., None], axis=2) / divisor).astype(jnp.bfloat16)
    pooled = pooled.reshape(samples, features * row_width)
    pooled_wide = pooled.astype(jnp.float32)
    upstream = cotangent[0].astype(jnp.float32)
    weighted = (upstream * pooled_wide).astype(jnp.bfloat16)
    low_term = jnp.dot(pooled, cross_down, preferred_element_type=jnp.float32)
    backward_term_part = jnp.dot(weighted, cross_up, preferred_element_type=jnp.float32)
    low_rank, back_rank = (
        lax.psum(low_term.astype(jnp.bfloat16), "mp").astype(jnp.float32),
        lax.psum(backward_term_part.astype(jnp.bfloat16), "mp").astype(jnp.float32),
    )
    rounded_low = low_rank.astype(jnp.bfloat16)
    rounded_back = back_rank.astype(jnp.bfloat16)
    scaled = (
        jnp.dot(rounded_low, cross_up.T, preferred_element_type=jnp.float32) + cross_bias[None, :]
    )
    crossed = (pooled_wide * scaled + pooled_wide).astype(jnp.bfloat16)
    pool_grad = (
        upstream * scaled
        + upstream
        + jnp.dot(rounded_back, cross_down.T, preferred_element_type=jnp.float32)
    )
    lookup_grad = (
        pool_grad.reshape(samples, features, 1, row_width)
        / divisor[..., None]
        * live_mask[..., None]
    ).astype(jnp.bfloat16)
    outgoing = jnp.zeros((arrived_flat.shape[0], row_width), jnp.bfloat16)
    outgoing = (
        outgoing.at[slot_index.reshape(-1)]
        .set(lookup_grad.reshape(-1, row_width))
        .reshape(arrived.shape)
    )
    returned = lax.all_to_all(outgoing, "mp", split_axis=0, concat_axis=0, tiled=True)
    row_grad = jax.ops.segment_sum(
        returned.reshape(-1, row_width).astype(jnp.float32),
        wanted.reshape(-1),
        num_segments=row_table.shape[0],
    )
    summed = lax.psum(row_grad, "replica")
    fresh_history_sums = grad_history + summed * summed
    new_table = row_table - learn_rate * summed / (jnp.sqrt(fresh_history_sums) + epsilon)
    return (crossed[None], new_table, fresh_history_sums)


def solution(mesh):
    in_specs = (
        P("mp", None),
        P("mp", None),
        P("replica", "mp", None, None),
        P("replica", None, "mp", None),
        P("replica", None, "mp"),
        P("mp", None),
        P("mp", None),
        P("mp"),
        P("replica", None, "mp"),
    )
    out_specs = (P("replica", None, "mp"), P("mp", None), P("mp", None))
    return jax.shard_map(shards, mesh=mesh, in_specs=in_specs, out_specs=out_specs, check_vma=False)
```

profile of v0, /device:TPU:0, one launch (start us, length us, event | category | flops | bytes accessed | tf_op | source)
XLA Modules:
  0.0 208.6 jit_solution(16695111438148539560)
XLA Ops:
  7.2 0.0 copy-start
  7.2 0.8 fusion.17
  8.0 1.3 convert_element_type.72
  9.2 8.1 %gather_fusion = bf16[2048,128]{1,0:T(8,128)(2,1)} fusion(bf16[2048,128]{1,0:T(8,128)(2,1)S(1)} %convert_element_type.72, s32[2048]{0:T(1024)S(1)} %broadcast_clamp_fusion.1), kind=kCustom, calls=%fused_computation | custom fusion | bytes 1056768 | tf_op jit(solution)/shard_map/gather | solution.py:23
  17.3 6.5 %all-to-all-start = ((bf16[8,256,128]{2,1,0:T(8,128)(2,1)}), bf16[8,256,128]{2,1,0:T(8,128)(2,1)S(1)}, u32[]{:S(2)}, u32[]{:S(2)}) async-start(bf16[8,256,128]{2,1,0:T(8,128)(2,1)} %bitcast.1), calls=%async_computation | async-start | bytes 1048576 | tf_op jit(solution)/shard_map/all_to_all | solution.py:24
  23.7 0.0 all-reduce.6.cloned.1.call-start
  23.8 0.0 copy-done.8
  23.8 0.1 copy.16
  24.0 0.1 copy.15
  24.1 0.3 fusion.8
  24.4 0.0 copy-start.6
  24.5 0.4 reshape.147
  24.9 0.2 copy-done.6
  25.1 0.3 copy.17
  25.4 0.3 copy.14
  25.7 0.4 reshape.159
  26.1 0.5 reshape_squeeze.3
  26.6 12.5 %all-to-all-done = bf16[8,256,128]{2,1,0:T(8,128)(2,1)S(1)} async-done(((bf16[8,256,128]{2,1,0:T(8,128)(2,1)}), bf16[8,256,128]{2,1,0:T(8,128)(2,1)S(1)}, u32[]{:S(2)}, u32[]{:S(2)}) %all-to-all-start) | async-done | bytes 524320 | tf_op jit(solution)/shard_map/all_to_all | solution.py:24
  39.1 6.2 %gather_fusion.1 = bf16[2048,128]{1,0:T(8,128)(2,1)S(1)} fusion(bf16[2048,128]{1,0:T(8,128)(2,1)S(1)} %bitcast.48, s32[2048]{0:T(1024)S(1)} %broadcast_clamp_fusion), kind=kCustom, calls=%fused_computation.1 | custom fusion | bytes 1056768 | tf_op jit(solution)/shard_map/gather | solution.py:29
  45.3 1.9 fusion.2
  47.2 0.0 copy-start.2
  47.2 0.3 divide_convert_fusion
  47.6 0.7 copy-done.2
  48.3 1.0 convolution_convert_fusion.1
  49.3 0.0 copy-done
  49.3 0.0 copy-done.4
  49.3 1.0 convolution_convert_fusion
  50.3 0.0 all-reduce.6.cloned.1.call-update
  50.3 0.0 copy-start.9
  50.3 55.4 %all-reduce.6.cloned.1.call-done = (bf16[256,512]{1,0:T(8,128)(2,1)}, bf16[256,512]{1,0:T(8,128)(2,1)}) async-done(((bf16[256,512]{1,0:T(8,128)(2,1)}, bf16[256,512]{1,0:T(8,128)(2,1)}), (bf16[256,512]{1,0:T(8,128)(2,1)}, bf16[256,512]{1,0:T(8,128)(2,1)})) %all-reduce.6.cloned.1.call-update) | async-done | bytes 524304 | tf_op jit(solution)/shard_map/psum | solution.py:42
  105.7 0.0 copy-done.9
  105.7 1.3 convolution_add_fusion.1
  107.0 0.0 copy-done.5
  107.0 0.3 convolution_add_fusion
  107.4 0.2 reshape.144
  107.6 0.3 broadcast_divide_fusion
  107.9 0.4 mul.47
  108.3 7.5 %scatter_custom_fusion = bf16[2048,128]{1,0:T(8,128)(2,1)} fusion(s32[2048]{0:T(1024)S(1)} %bitcast.58, f32[2048,128]{1,0:T(8,128)S(1)} %bitcast.49, f32[2048]{0:T(1024)S(1)} %reshape.147, bf16[]{:T(256)} %constant.9.clone.1), kind=kCustom, calls=%fused_computation.21 | custom fusion | flops 524288 | bytes 1581058 | tf_op jit(solution)/shard_map/scatter | solution.py:64
  115.8 3.6 %all-to-all-start.1 = ((bf16[8,256,128]{2,1,0:T(8,128)(2,1)}), bf16[8,256,128]{2,1,0:T(8,128)(2,1)S(1)}, u32[]{:S(2)}, u32[]{:S(2)}) async-start(bf16[8,256,128]{2,1,0:T(8,128)(2,1)} %bitcast.11), calls=%async_computation.1 | async-start | bytes 1048576 | tf_op jit(solution)/shard_map/all_to_all | solution.py:67
  119.4 0.0 all-reduce.4.cloned.1.call-start
  119.5 0.0 copy-done.7
  119.5 15.2 %all-to-all-done.1 = bf16[8,256,128]{2,1,0:T(8,128)(2,1)S(1)} async-done(((bf16[8,256,128]{2,1,0:T(8,128)(2,1)}), bf16[8,256,128]{2,1,0:T(8,128)(2,1)S(1)}, u32[]{:S(2)}, u32[]{:S(2)}) %all-to-all-start.1) | async-done | bytes 524320 | tf_op jit(solution)/shard_map/all_to_all | solution.py:67
  134.7 12.5 %scatter_custom_fusion.1 = f32[2048,128]{1,0:T(8,128)} fusion(s32[2048]{0:T(1024)S(1)} %bitcast.59, bf16[2048,128]{1,0:T(8,128)(2,1)S(1)} %bitcast.54, f32[]{:T(128)} %constant.8.clone.1), kind=kCustom, calls=%fused_computation.8 | custom fusion | flops 524288 | bytes 1572868 | tf_op jit(solution)/shard_map/scatter-add | solution.py:68
  147.2 0.0 all-reduce.4.cloned.1.call-update
  147.2 0.8 fusion.10
  148.0 50.7 %all-reduce.4.cloned.1.call-done = f32[2048,128]{1,0:T(8,128)} async-done(((f32[2048,128]{1,0:T(8,128)}), f32[2048,128]{1,0:T(8,128)}) %all-reduce.4.cloned.1.call-update) | async-done | bytes 1048592 | tf_op jit(solution)/shard_map/psum | solution.py:73
  198.7 0.0 copy-done.1
  198.7 3.0 %divide_subtract_fusion = (f32[2048,128]{1,0:T(8,128)}, f32[2048,128]{1,0:T(8,128)}) fusion(f32[2048,128]{1,0:T(8,128)S(1)} %copy-done.1, f32[2048,128]{1,0:T(8,128)} %all-reduce.4.cloned.1.call-done, f32[2048,128]{1,0:T(8,128)S(1)} %copy-done.3), kind=kLoop, calls=%fused_computation.12 | loop fusion | flops 1572864 | bytes 5242880 | tf_op jit(solution)/shard_map/sub | solution.py:75
  (14 shorter events, 0.1 us)
Async XLA Ops:
  7.2 42.1 %copy-start = (bf16[512,512]{1,0:T(8,128)(2,1)S(1)}, bf16[512,512]{1,0:T(8,128)(2,1)}, u32[]{:S(2)}) copy-start(bf16[512,512]{1,0:T(8,128)(2,1)} %param.15) | copy-start | bytes 1572868
  17.3 6.5 %copy-start.8 = (s32[1,256,4]{1,2,0:T(4,128)S(1)}, s32[1,256,4]{1,2,0:T(4,128)}, u32[]{:S(2)}) copy-start(s32[1,256,4]{1,2,0:T(4,128)} %param.13) | copy-start | bytes 12292
  17.3 21.8 %all-to-all-start = ((bf16[8,256,128]{2,1,0:T(8,128)(2,1)}), bf16[8,256,128]{2,1,0:T(8,128)(2,1)S(1)}, u32[]{:S(2)}, u32[]{:S(2)}) async-start(bf16[8,256,128]{2,1,0:T(8,128)(2,1)} %bitcast.1), calls=%async_computation | async-start | bytes 1048576 | tf_op jit(solution)/shard_map/all_to_all | solution.py:24
  23.7 81.9 %all-reduce.6.cloned.1.call-start = ((), (), s32[]{:S(2)}) async-start(), calls=%async_computation.3 | async-start | bytes 1048576 | tf_op jit(solution)/shard_map/psum | solution.py:42
  24.4 0.7 copy-start.6
  47.2 1.0 copy-start.2
  48.3 1.0 copy-start.4
  50.3 55.4 %copy-start.9 = (f32[512]{0:T(512)S(1)}, f32[512]{0:T(512)}, u32[]{:S(2)}) copy-start(f32[512]{0:T(512)} %param.16) | copy-start | bytes 6148
  105.7 1.3 copy-start.5
  115.8 3.7 %copy-start.7 = (s32[1,1,8,256]{3,2,1,0:T(8,128)S(1)}, s32[1,1,8,256]{3,2,1,0:T(8,128)}, u32[]{:S(2)}) copy-start(s32[1,1,8,256]{3,2,1,0:T(8,128)} %param.11) | copy-start | bytes 24580
  115.8 18.9 %all-to-all-start.1 = ((bf16[8,256,128]{2,1,0:T(8,128)(2,1)}), bf16[8,256,128]{2,1,0:T(8,128)(2,1)S(1)}, u32[]{:S(2)}, u32[]{:S(2)}) async-start(bf16[8,256,128]{2,1,0:T(8,128)(2,1)} %bitcast.11), calls=%async_computation.1 | async-start | bytes 1048576 | tf_op jit(solution)/shard_map/all_to_all | solution.py:67
  119.4 79.3 %all-reduce.4.cloned.1.call-start = ((), (), s32[]{:S(2)}) async-start(), calls=%async_computation.2 | async-start | bytes 2097152 | tf_op jit(solution)/shard_map/psum | solution.py:73
  147.2 51.6 %copy-start.1 = (f32[2048,128]{1,0:T(8,128)S(1)}, f32[2048,128]{1,0:T(8,128)}, u32[]{:S(2)}) copy-start(f32[2048,128]{1,0:T(8,128)} %param.9) | copy-start | bytes 3145732
  147.2 51.6 %copy-start.3 = (f32[2048,128]{1,0:T(8,128)S(1)}, f32[2048,128]{1,0:T(8,128)}, u32[]{:S(2)}) copy-start(f32[2048,128]{1,0:T(8,128)} %param.10) | copy-start | bytes 3145732
Sparse Core Ops, SparseCore 0:
  50.4 55.2 all-reduce.5
  147.3 51.3 all-reduce.3
where the time goes:
time: 209 us
  waiting for transfers between devices  134 us (64%)
  other arithmetic  28.8 us (14%)
  local copies, waits for them, and re-layouts  17.9 us (9%)
  between operations  14.3 us (7%)
  starting transfers between devices  10.2 us (5%)
  matrix products  3.67 us (2%)
    psum x1, waiting for transfers between devices, shards(): lax.psum(low_term.astype(jnp.bfloat16), 'mp').astype(jnp.float32)  55.4 us
    psum x1, waiting for transfers between devices, shards(): summed = lax.psum(row_grad, 'replica')  50.7 us
    all_to_all x1, waiting for transfers between devices, shards(): lax.all_to_all(outgoing, 'mp', split_axis=0, concat_axis=0, tiled=True)  15.2 us
    scatter-add x1, other arithmetic, shards(): jax.ops.segment_sum(returned.reshape(-1, row_width).astype(jnp.float32),...  12.5 us
    all_to_all x1, waiting for transfers between devices, shards(): lax.all_to_all(sending, 'mp', split_axis=0, concat_axis=0, tiled=True)  12.5 us
    gather x1, local copies, waits for them, and re-layouts, shards(): sending = row_table.astype(jnp.bfloat16)[wanted]  8.05 us
    scatter x1, other arithmetic, shards(): outgoing = outgoing.at[slot_index.reshape(-1)].set(lookup_grad.reshape(-1...  7.48 us
    all_to_all x1, starting transfers between devices, shards(): lax.all_to_all(sending, 'mp', split_axis=0, concat_axis=0, tiled=True)  6.46 us
  transfers between devices with their start and end apart: 4, of which 4 were waited for; matrix products, arithmetic and copies ran while one was open for 2% of the time, Pallas kernels for 0%

commit v1 on v0

v1 whole, which is shorter than its diff:
```python
import functools

import jax
import jax.numpy as jnp
from jax import lax
from jax.experimental import pallas as pl
from jax.experimental.pallas import tpu as pltpu
from jax.sharding import PartitionSpec as P

learn_rate = 0.5
epsilon = 1e-06
LANES = 128
bf16 = jnp.bfloat16
f32 = jnp.float32


def flip(index, distance, count):
    result = 0
    bit = 1
    while bit < count:
        result = result + bit * lax.rem(
            lax.div(jnp.int32(index), jnp.int32(bit)) + lax.div(jnp.int32(distance), jnp.int32(bit)),
            jnp.int32(2),
        )
        bit *= 2
    return result


def steps(order, body):
    if len(order) <= 8:
        for d in order:
            body(d)
    else:
        first, stride = order[0], order[1] - order[0]
        lax.fori_loop(0, len(order), lambda i, c: (body(first + stride * i), c)[1], 0)


def ones_where(mask):
    return jnp.where(mask, 1.0, 0.0).astype(bf16)


def kernel(
    n,
    nr,
    table_ref,
    wanted_ref,
    slots_ref,
    counts_ref,
    down_ref,
    up_ref,
    bias_ref,
    cot_ref,
    crossed_ref,
    grad_ref,
    table_half,
    onehot,
    rows_out,
    rows_in,
    columns,
    pick,
    place,
    owned,
    pool_sum,
    pooled_half,
    weighted,
    part,
    part_in,
    reduced,
    full,
    grad_half,
    grads_out,
    grads_in,
    row_sum,
    row_part,
    row_part_in,
    row_reduced,
    row_full,
    rows_send,
    rows_recv,
    part_send,
    part_recv,
    full_send,
    full_recv,
    grads_send,
    grads_recv,
    row_part_send,
    row_part_recv,
    row_full_send,
    row_full_recv,
):
    me = lax.axis_index("mp")
    group = lax.axis_index("replica")
    cap = wanted_ref.shape[1]
    rows, width = table_ref.shape
    samples, features = counts_ref.shape
    hot = slots_ref.shape[0] // features
    rank = down_ref.shape[1]
    piece = min(cap, LANES)
    near = list(range(1, n))
    far = near[::-1]
    group_far = list(range(nr - 1, 0, -1))

    barrier = pltpu.get_barrier_semaphore()
    for_mp = lambda d: pl.semaphore_signal(
        barrier, inc=1, device_id={"mp": flip(me, d, n)}, device_id_type=pl.DeviceIdType.MESH
    )
    for_replica = lambda e: pl.semaphore_signal(
        barrier, inc=1, device_id={"replica": flip(group, e, nr)}, device_id_type=pl.DeviceIdType.MESH
    )
    steps(far, for_mp)
    steps(group_far, for_replica)

    def to_mp(src, dst, send, recv, d):
        return pltpu.make_async_remote_copy(
            src_ref=src,
            dst_ref=dst,
            send_sem=send.at[d],
            recv_sem=recv.at[d],
            device_id={"mp": flip(me, d, n)},
            device_id_type=pl.DeviceIdType.MESH,
        )

    def to_replica(src, dst, send, recv, e):
        return pltpu.make_async_remote_copy(
            src_ref=src,
            dst_ref=dst,
            send_sem=send.at[e],
            recv_sem=recv.at[e],
            device_id={"replica": flip(group, e, nr)},
            device_id_type=pl.DeviceIdType.MESH,
        )

    rows_copy = lambda d: to_mp(rows_out.at[d], rows_in.at[d], rows_send, rows_recv, d)
    part_copy = lambda d: to_mp(
        part.at[flip(me, d, n)], part_in.at[d], part_send, part_recv, d
    )
    full_copy = lambda d: to_mp(reduced, full.at[me], full_send, full_recv, d)
    grads_copy = lambda d: to_mp(grads_out.at[d], grads_in.at[d], grads_send, grads_recv, d)
    row_part_copy = lambda e: to_replica(
        row_part.at[flip(group, e, nr)], row_part_in.at[e], row_part_send, row_part_recv, e
    )
    row_full_copy = lambda e: to_replica(
        row_reduced, row_full.at[group], row_full_send, row_full_recv, e
    )

    table_half[...] = table_ref[...].astype(bf16)
    lane = lax.broadcasted_iota(jnp.int32, (cap, LANES), 1)

    def gather(d):
        row = wanted_ref[pl.ds(flip(me, d, n), 1), :]
        column = jnp.broadcast_to(row, (LANES, cap)).T
        for j in range(rows // LANES):
            onehot[:, j * LANES : (j + 1) * LANES] = ones_where(column == lane + j * LANES)
        return jnp.dot(onehot[...], table_half[...], preferred_element_type=f32).astype(bf16)

    rows_in[0] = gather(0)
    pl.semaphore_wait(barrier, n - 1 + nr - 1)

    def send_rows(d):
        rows_out[d] = gather(d)
        rows_copy(d).start()

    steps(far, send_rows)

    for i in range(hot * features):
        columns[i] = jnp.broadcast_to(slots_ref[i : i + 1, :], (LANES, samples)).T
    piece_lane = lax.broadcasted_iota(jnp.int32, (samples, piece), 1)
    cap_row = lax.broadcasted_iota(jnp.int32, (cap, samples), 0)
    block_row = lax.broadcasted_iota(jnp.int32, (LANES, cap), 0)

    def build_pick(d):
        base = flip(me, d, n) * cap
        for f in range(features):
            for j in range(cap // piece):
                mask = None
                for k in range(hot):
                    hit = columns[k * features + f][:, :piece] - (base + j * piece) == piece_lane
                    mask = hit if mask is None else mask | hit
                pick[d, f * samples : (f + 1) * samples, j * piece : (j + 1) * piece] = ones_where(mask)

    def build_place(d):
        base = flip(me, d, n) * cap
        for f in range(features):
            mask = None
            for k in range(hot):
                i = k * features + f
                hit = slots_ref[i : i + 1, :] - base == cap_row
                mask = hit if mask is None else mask | hit
            place[d, :, f * samples : (f + 1) * samples] = ones_where(mask)

    def build_owned(d):
        row = wanted_ref[pl.ds(flip(me, d, n), 1), :]
        for j in range(rows // LANES):
            owned[d, j * LANES : (j + 1) * LANES, :] = ones_where(row == block_row + j * LANES)

    steps([0] + near, build_pick)
    pool_sum[...] = jnp.dot(pick[0], rows_in[0], preferred_element_type=f32)
    steps([0] + near, build_place)
    steps([0] + near, build_owned)

    def pool(d):
        rows_copy(d).wait_recv()
        pool_sum[...] += jnp.dot(pick[d], rows_in[d], preferred_element_type=f32)

    steps(near, pool)

    for f in range(features):
        cut = slice(f * width, (f + 1) * width)
        divisor = counts_ref[:, f : f + 1].astype(f32)
        value = (pool_sum[f * samples : (f + 1) * samples, :] / divisor).astype(bf16)
        pooled_half[:, cut] = value
        weighted[:, cut] = (cot_ref[:, cut].astype(f32) * value.astype(f32)).astype(bf16)
    low = jnp.dot(pooled_half[...], down_ref[...], preferred_element_type=f32)
    part[:, :, :rank] = low.reshape(n, samples // n, rank).astype(bf16)
    back = jnp.dot(weighted[...], up_ref[...], preferred_element_type=f32)
    part[:, :, rank:] = back.reshape(n, samples // n, rank).astype(bf16)

    steps(far, lambda d: part_copy(d).start())
    total = part[me].astype(f32)
    if n <= 8:
        for d in near:
            part_copy(d).wait_recv()
            total = total + part_in[d].astype(f32)
    else:

        def add(i, value):
            part_copy(i + 1).wait_recv()
            return value + part_in[i + 1].astype(f32)

        total = lax.fori_loop(0, n - 1, add, total)
    reduced[...] = total.astype(bf16)
    steps(far, lambda d: full_copy(d).start())
    full[me] = reduced[...]
    steps(near, lambda d: full_copy(d).wait_recv())

    low_half = full[:, :, :rank].reshape(samples, rank)
    back_half = full[:, :, rank:].reshape(samples, rank)
    transposed = (((1,), (1,)), ((), ()))
    for f in range(features):
        cut = slice(f * width, (f + 1) * width)
        scaled = (
            lax.dot_general(low_half, up_ref[cut, :], transposed, preferred_element_type=f32)
            + bias_ref[:, cut]
        )
        wide = pooled_half[:, cut].astype(f32)
        crossed_ref[:, cut] = (wide * scaled + wide).astype(bf16)
        upstream = cot_ref[:, cut].astype(f32)
        pool_grad = (
            upstream * scaled
            + upstream
            + lax.dot_general(back_half, down_ref[cut, :], transposed, preferred_element_type=f32)
        )
        divisor = counts_ref[:, f : f + 1].astype(f32)
        grad_half[f * samples : (f + 1) * samples, :] = (pool_grad / divisor).astype(bf16)

    def send_grads(d):
        grads_out[d] = jnp.dot(place[d], grad_half[...], preferred_element_type=f32).astype(bf16)
        grads_copy(d).start()

    steps(far, send_grads)
    grads_in[0] = jnp.dot(place[0], grad_half[...], preferred_element_type=f32).astype(bf16)
    row_sum[...] = jnp.dot(owned[0], grads_in[0], preferred_element_type=f32)

    def collect(d):
        grads_copy(d).wait_recv()
        row_sum[...] += jnp.dot(owned[d], grads_in[d], preferred_element_type=f32)

    steps(near, collect)

    row_part[...] = row_sum[...].reshape(row_part.shape).astype(bf16)
    steps(group_far, lambda e: row_part_copy(e).start())
    total = row_part[group].astype(f32)
    if nr <= 8:
        for e in group_far[::-1]:
            row_part_copy(e).wait_recv()
            total = total + row_part_in[e].astype(f32)
    else:

        def add_rows(i, value):
            row_part_copy(i + 1).wait_recv()
            return value + row_part_in[i + 1].astype(f32)

        total = lax.fori_loop(0, nr - 1, add_rows, total)
    row_reduced[...] = total.astype(bf16)
    steps(group_far, lambda e: row_full_copy(e).start())
    row_full[group] = row_reduced[...]
    steps(group_far[::-1], lambda e: row_full_copy(e).wait_recv())
    grad_ref[...] = row_full[...].reshape(rows, width)

    steps(near, lambda d: rows_copy(d).wait_send())
    steps(near, lambda d: part_copy(d).wait_send())
    steps(near, lambda d: full_copy(d).wait_send())
    steps(near, lambda d: grads_copy(d).wait_send())
    steps(group_far, lambda e: row_part_copy(e).wait_send())
    steps(group_far, lambda e: row_full_copy(e).wait_send())


def shards(
    n,
    nr,
    row_table,
    grad_history,
    touched,
    lookup_slot,
    pool_counts,
    cross_down,
    cross_up,
    cross_bias,
    cotangent,
):
    rows, width = row_table.shape
    wanted = touched[0, 0]
    cap = wanted.shape[1]
    counts = pool_counts[0]
    slot_index = lookup_slot[0]
    samples, features, hot = slot_index.shape
    rank = cross_down.shape[1]
    live = jnp.arange(hot, dtype=jnp.int32)[None, None, :] < counts[:, :, None]
    slots = jnp.where(live, slot_index, -1).transpose(2, 1, 0).reshape(hot * features, samples)
    dma = pltpu.SemaphoreType.DMA
    vmem = pl.BlockSpec(memory_space=pltpu.VMEM)
    lookups = features * samples
    crossed, summed = pl.pallas_call(
        functools.partial(kernel, n, nr),
        out_shape=(
            jax.ShapeDtypeStruct((samples, features * width), bf16),
            jax.ShapeDtypeStruct((rows, width), bf16),
        ),
        in_specs=[vmem] * 8,
        out_specs=(vmem, vmem),
        scratch_shapes=[
            pltpu.VMEM((rows, width), bf16),
            pltpu.VMEM((cap, rows), bf16),
            pltpu.VMEM((n, cap, width), bf16),
            pltpu.VMEM((n, cap, width), bf16),
            pltpu.VMEM((hot * features, samples, LANES), jnp.int32),
            pltpu.VMEM((n, lookups, cap), bf16),
            pltpu.VMEM((n, cap, lookups), bf16),
            pltpu.VMEM((n, rows, cap), bf16),
            pltpu.VMEM((lookups, width), f32),
            pltpu.VMEM((samples, features * width), bf16),
            pltpu.VMEM((samples, features * width), bf16),
            pltpu.VMEM((n, samples // n, 2 * rank), bf16),
            pltpu.VMEM((n, samples // n, 2 * rank), bf16),
            pltpu.VMEM((samples // n, 2 * rank), bf16),
            pltpu.VMEM((n, samples // n, 2 * rank), bf16),
            pltpu.VMEM((lookups, width), bf16),
            pltpu.VMEM((n, cap, width), bf16),
            pltpu.VMEM((n, cap, width), bf16),
            pltpu.VMEM((rows, width), f32),
            pltpu.VMEM((nr, rows // nr, width), bf16),
            pltpu.VMEM((nr, rows // nr, width), bf16),
            pltpu.VMEM((rows // nr, width), bf16),
            pltpu.VMEM((nr, rows // nr, width), bf16),
        ]
        + [dma((n,))] * 8
        + [dma((nr,))] * 4,
        compiler_params=pltpu.CompilerParams(
            collective_id=0, has_side_effects=True, vmem_limit_bytes=56 * 1024 * 1024
        ),
        cost_estimate=pl.CostEstimate(flops=10**9 * 6, bytes_accessed=10**7, transcendentals=0),
    )(row_table, wanted, slots, counts, cross_down, cross_up, cross_bias[None, :], cotangent[0])
    summed = summed.astype(f32)
    fresh_history_sums = grad_history + summed * summed
    new_table = row_table - learn_rate * summed / (jnp.sqrt(fresh_history_sums) + epsilon)
    return (crossed[None], new_table, fresh_history_sums)


def solution(mesh):
    in_specs = (
        P("mp", None),
        P("mp", None),
        P("replica", "mp", None, None),
        P("replica", None, "mp", None),
        P("replica", None, "mp"),
        P("mp", None),
        P("mp", None),
        P("mp"),
        P("replica", None, "mp"),
    )
    out_specs = (P("replica", None, "mp"), P("mp", None), P("mp", None))
    body = functools.partial(shards, mesh.shape["mp"], mesh.shape["replica"])
    return jax.shard_map(body, mesh=mesh, in_specs=in_specs, out_specs=out_specs, check_vma=False)
```

time: 209 us -> 82.2 us (0.39)
  waiting for transfers between devices: 134 us -> 0 us
  Pallas kernels: 0 us -> 75.3 us
  other arithmetic: 28.8 us -> 2.91 us
  local copies, waits for them, and re-layouts: 17.9 us -> 2.86 us
  between operations: 14.3 us -> 0.7 us
  starting transfers between devices: 10.2 us -> 0 us
  matrix products: 3.67 us -> 0 us
    psum x2 -> x0, waiting for transfers between devices: 106 us -> none  [the longest x1 55.4 us: shards(): lax.psum(low_term.astype(jnp.bfloat16), 'mp').astype(jnp.float32)]
    pallas_call x0 -> x1, Pallas kernels: none -> 75.3 us  [shards(): pl.pallas_call(functools.partial(kernel, n, nr), out_shape=(jax.ShapeDtyp...]
    all_to_all x2 -> x0, waiting for transfers between devices: 27.7 us -> none  [the longest x1 15.2 us: shards(): lax.all_to_all(outgoing, 'mp', split_axis=0, concat_axis=0, tiled=True)]
    gather x2 -> x0, local copies, waits for them, and re-layouts: 14.2 us -> none  [the longest x1 8.05 us: shards(): sending = row_table.astype(jnp.bfloat16)[wanted]]
    scatter-add x1 -> x0, other arithmetic: 12.5 us -> none  [shards(): jax.ops.segment_sum(returned.reshape(-1, row_width).astype(jnp.float32),...]
    all_to_all x2 -> x0, starting transfers between devices: 10.1 us -> none  [the longest x1 6.46 us: shards(): lax.all_to_all(sending, 'mp', split_axis=0, concat_axis=0, tiled=True)]
    scatter x1 -> x0, other arithmetic: 7.48 us -> none  [shards(): outgoing = outgoing.at[slot_index.reshape(-1)].set(lookup_grad.reshape(-1...]
    dot_general x4 -> x0, matrix products: 3.67 us -> none  [the longest x1 1.32 us: shards(): jnp.dot(rounded_low, cross_up.T, preferred_element_type=jnp.float32)]
  transfers between devices with their start and end apart: 4 -> 0, of which waited for: 4 -> 0; matrix products, arithmetic and copies ran while one was open for 2% -> 0% of each run, Pallas kernels for 0% -> 0%
where the time goes in v1:
time: 82.2 us; the launch traced here: 81.8 us
  Pallas kernels  75.3 us (92%)
  other arithmetic  2.91 us (4%)
  local copies, waits for them, and re-layouts  2.86 us (3%)
    pallas_call x1, Pallas kernels, shards(): pl.pallas_call(functools.partial(kernel, n, nr), out_shape=(jax.ShapeDtyp...  75.3 us
    sub x1, other arithmetic, shards(): row_table - learn_rate * summed / (jnp.sqrt(fresh_history_sums) + epsilon)  2.9 us
    unnamed x14, local copies, waits for them, and re-layouts  2.17 us

profile of v1, /device:TPU:0, one launch (start us, length us, event | category | flops | bytes accessed | tf_op | source)
XLA Modules:
  0.0 81.8 jit_solution(9814583775478873086)
XLA Ops:
  0.6 0.0 copy-start.5
  0.6 0.7 copy-done.5
  1.3 0.1 copy.12
  1.5 0.0 copy-start.2
  1.5 0.0 copy-start.4
  1.5 0.1 copy.13
  1.6 0.6 copy-done.4
  2.2 0.6 reshape.10.slots_ref
  2.8 0.0 copy-done.2
  2.8 0.0 copy-start
  2.8 0.0 copy-start.1
  2.8 75.3 %shard_map.112 = (bf16[256,512]{1,0:T(8,128)(2,1)}, bf16[2048,128]{1,0:T(8,128)(2,1)}) custom-call(f32[2048,128]{1,0:T(8,128)} %table_ref.1, s32[8,256]{1,0:T(8,128)} %bitcast.13, s32[8,256]{1,0:T(8,128)} %reshape.10.slots_ref, s32[256,4]{1,0:T(8,128)} %bitcast.10, bf16[512,512]{1,0:T(8,128)(2,1)} %down_ref.1, bf16[512,512]{1,0:T(8,128)(2,1)} %up_ref.1, ...), custom_call_target="tpu_custom_call" | custom-call | flops 6000000000 | bytes 10000000 | tf_op jit(solution)/shard_map/pallas_call | solution.py:323
  78.2 0.0 copy-done
  78.2 0.0 copy-done.1
  78.2 0.0 copy-start.3
  78.2 2.9 %fusion.1 = (f32[2048,128]{1,0:T(8,128)}, f32[2048,128]{1,0:T(8,128)}) fusion(f32[2048,128]{1,0:T(8,128)S(1)} %copy-done, bf16[2048,128]{1,0:T(8,128)(2,1)} %get-tuple-element.6, f32[2048,128]{1,0:T(8,128)S(1)} %copy-done.1), kind=kLoop, calls=%fused_computation.3 | loop fusion | flops 1835008 | bytes 4718592 | tf_op jit(solution)/shard_map/sub | solution.py:365
  81.1 0.0 copy-done.3
  81.1 0.7 copy.16
  (2 shorter events, 0.0 us)
Async XLA Ops:
  0.6 0.7 copy-start.5
  1.5 1.4 %copy-start.2 = (s32[1,256,4]{2,1,0:T(8,128)}, s32[1,256,4]{2,1,0:T(8,128)S(1)}, u32[]{:S(2)}) copy-start(s32[1,256,4]{2,1,0:T(8,128)S(1)} %copy.12) | copy-start | bytes 12292
  1.5 0.7 copy-start.4
  2.8 75.3 %copy-start = (f32[2048,128]{1,0:T(8,128)S(1)}, f32[2048,128]{1,0:T(8,128)}, u32[]{:S(2)}) copy-start(f32[2048,128]{1,0:T(8,128)} %table_ref.1) | copy-start | bytes 3145732
  2.8 75.4 %copy-start.1 = (f32[2048,128]{1,0:T(8,128)S(1)}, f32[2048,128]{1,0:T(8,128)}, u32[]{:S(2)}) copy-start(f32[2048,128]{1,0:T(8,128)} %param.10) | copy-start | bytes 3145732
  78.2 2.9 %copy-start.3 = (bf16[256,512]{1,0:T(8,128)(2,1)S(1)}, bf16[256,512]{1,0:T(8,128)(2,1)}, u32[]{:S(2)}) copy-start(bf16[256,512]{1,0:T(8,128)(2,1)} %get-tuple-element.5) | copy-start | bytes 786436
